TPU v7x, 128 devices: a whole 4x4x4 slice. The times are simulated.
128 devices in a mesh: dp: 8 (over y_lo, x), tensor: 16 (over y_hi, z, core).
Axes of the slice: x: 4, y: 4 (y_hi: 2, y_lo: 2; y = y_hi * 2 + y_lo), z: 4, core: 2. Of those that a mesh axis runs over, the one named last changes fastest.
Arguments:
- tokens: bfloat16 [2048, 4096], P(('dp', 'tensor')), may hold values from -6 to 6
- rms_norm_gain: bfloat16 [4096], replicated, may hold values from 0.5 to 2
- w_gate: bfloat16 [4096, 14336], P(None, 'tensor'), may hold values from -0.09375 to 0.09375
- w_up: bfloat16 [4096, 14336], P(None, 'tensor'), may hold values from -0.09375 to 0.09375
- w_down: bfloat16 [14336, 4096], P('tensor'), may hold values from -0.046875 to 0.046875
- output_cotangent: bfloat16 [2048, 4096], P(('dp', 'tensor')), may hold values from -6 to 6
Outputs:
- layer_out: bfloat16 [2048, 4096], P(('dp', 'tensor'))
- token_input_gradient: bfloat16 [2048, 4096], P(('dp', 'tensor'))
- grad_gate: bfloat16 [4096, 14336], P('dp', 'tensor')
- grad_up: bfloat16 [4096, 14336], P('dp', 'tensor')
- grad_down: bfloat16 [14336, 4096], P('tensor', 'dp')
All inputs are finite; a program needn't handle non-finite values.
Results may differ from a plain program's by a relative error of at most 0.019.
Values may be sent and summed in bfloat16 or wider, within the bound.
A program may use at most 192 MiB of HBM per device.

v0:
```python
import jax
import jax.numpy as jnp
from jax import lax
from jax.sharding import PartitionSpec as P


def project(normed_full, w_gate, w_up):
    gate = jnp.dot(normed_full, w_gate, preferred_element_type=jnp.float32)
    up = jnp.dot(normed_full, w_up, preferred_element_type=jnp.float32)
    return (gate, up)


def first_dim_product(left, right):
    return lax.dot_general(
        left, right, (((0,), (0,)), ((), ())), preferred_element_type=jnp.float32
    )


def last_dim_product(left, right):
    return lax.dot_general(
        left, right, (((1,), (1,)), ((), ())), preferred_element_type=jnp.float32
    )


def local(tokens, rms_norm_gain, w_gate, w_up, w_down, output_cotangent):
    input_float = tokens.astype(jnp.float32)
    reciprocal_scale = lax.rsqrt(
        jnp.mean(input_float * input_float, axis=-1, keepdims=True) + 1e-05
    )
    normalized_input = input_float * reciprocal_scale
    gain_float = rms_norm_gain.astype(jnp.float32)
    normalized_tokens = (normalized_input * gain_float).astype(jnp.bfloat16)
    normed_full = lax.all_gather(normalized_tokens, "tensor", axis=0, tiled=True)
    gate, up = project(normed_full, w_gate, w_up)
    sig = jax.nn.sigmoid(gate)
    act = gate * sig
    hidden = (act * up).astype(jnp.bfloat16)
    summed = lax.psum_scatter(
        jnp.dot(hidden, w_down, preferred_element_type=jnp.float32).astype(jnp.bfloat16),
        "tensor",
        scatter_dimension=0,
        tiled=True,
    ).astype(jnp.float32)
    layer_out = (input_float + summed).astype(jnp.bfloat16)
    cot_full = lax.all_gather(output_cotangent, "tensor", axis=0, tiled=True)
    normed_use = lax.all_gather(normalized_tokens, "tensor", axis=0, tiled=True)
    gate_b, up_b = project(normed_use, w_gate, w_up)
    sig_b = jax.nn.sigmoid(gate_b)
    act_b = gate_b * sig_b
    hidden_b = (act_b * up_b).astype(jnp.bfloat16)
    d_hidden = last_dim_product(cot_full, w_down)
    d_gate = (d_hidden * up_b * sig_b * (1.0 + gate_b * (1.0 - sig_b))).astype(jnp.bfloat16)
    d_up = (d_hidden * act_b).astype(jnp.bfloat16)
    d_normed = lax.psum_scatter(
        (last_dim_product(d_gate, w_gate) + last_dim_product(d_up, w_up)).astype(jnp.bfloat16),
        "tensor",
        scatter_dimension=0,
        tiled=True,
    ).astype(jnp.float32)
    gain_scaled_gradient = d_normed * gain_float
    inner_product_sum = jnp.mean(gain_scaled_gradient * normalized_input, axis=-1, keepdims=True)
    token_input_gradient = (
        output_cotangent.astype(jnp.float32)
        + reciprocal_scale * (gain_scaled_gradient - normalized_input * inner_product_sum)
    ).astype(jnp.bfloat16)
    grad_gate = lax.psum_scatter(
        first_dim_product(normed_use, d_gate).astype(jnp.bfloat16),
        "dp",
        scatter_dimension=0,
        tiled=True,
    )
    grad_up = lax.psum_scatter(
        first_dim_product(normed_use, d_up).astype(jnp.bfloat16),
        "dp",
        scatter_dimension=0,
        tiled=True,
    )
    grad_down_t = lax.psum_scatter(
        first_dim_product(cot_full, hidden_b).astype(jnp.bfloat16),
        "dp",
        scatter_dimension=0,
        tiled=True,
    )
    return (layer_out, token_input_gradient, grad_gate, grad_up, grad_down_t.T)


def solution(mesh):
    placed = (
        P(("dp", "tensor"), None),
        P(),
        P(None, "tensor"),
        P(None, "tensor"),
        P("tensor", None),
        P(("dp", "tensor"), None),
    )
    return jax.shard_map(
        local,
        mesh=mesh,
        in_specs=placed,
        out_specs=(
            P(("dp", "tensor"), None),
            P(("dp", "tensor"), None),
            P("dp", "tensor"),
            P("dp", "tensor"),
            P("tensor", "dp"),
        ),
        check_vma=False,
    )
```

profile of v0, /device:TPU:0, one launch (start us, length us, event | category | flops | bytes accessed | tf_op | source)
XLA Modules:
  0.0 531.1 jit_solution(7939002043280490080)
XLA Ops:
  7.2 0.0 all-gather.3.cloned.1.call-start
  7.2 1.1 fusion.11
  8.3 0.7 convert_element_type.53
  9.0 1.7 fusion.5
  10.6 0.0 all-gather.3.cloned.1.call-update
  10.7 0.0 all-gather.5.cloned.1.call-start
  10.7 0.7 all-gather.5.cloned.1.call-update
  11.4 0.0 reduce-scatter.8.cloned.1.call-start
  11.5 49.7 %all-gather.3.cloned.1.call-done = bf16[256,4096]{1,0:T(8,128)(2,1)} async-done(((bf16[16,4096]{1,0:T(8,128)(2,1)}), bf16[256,4096]{1,0:T(8,128)(2,1)}) %all-gather.3.cloned.1.call-update) | async-done | bytes 2097168 | tf_op jit(solution)/shard_map/all_gather | solution.py:33
  61.2 7.1 %fusion.14 = f32[256,896]{1,0:T(8,128)} fusion(bf16[256,4096]{1,0:T(8,128)(2,1)} %all-gather.3.cloned.1.call-done, bf16[4096,896]{1,0:T(8,128)(2,1)} %param.9), kind=kOutput, calls=%fused_computation.29 | convolution fusion | flops 1879048192 | bytes 10354688 | tf_op jit(solution)/shard_map/dot_general | solution.py:9
  68.3 6.3 %fusion.13 = f32[256,896]{1,0:T(8,128)} fusion(bf16[256,4096]{1,0:T(8,128)(2,1)S(1)} %copy-done, bf16[4096,896]{1,0:T(8,128)(2,1)} %param.8), kind=kOutput, calls=%fused_computation.28 | convolution fusion | flops 1879048192 | bytes 10354688 | tf_op jit(solution)/shard_map/dot_general | solution.py:8
  74.6 35.4 %all-gather.5.cloned.1.call-done = bf16[256,4096]{1,0:T(8,128)(2,1)} async-done(((bf16[16,4096]{1,0:T(8,128)(2,1)}), bf16[256,4096]{1,0:T(8,128)(2,1)}) %all-gather.5.cloned.1.call-update) | async-done | bytes 2097168 | tf_op jit(solution)/shard_map/all_gather | solution.py:45
  110.0 6.9 %multiply_convert_fusion = (bf16[256,896]{1,0:T(8,128)(2,1)S(1)}, bf16[256,896]{1,0:T(8,128)(2,1)S(1)}, bf16[256,896]{1,0:T(8,128)(2,1)S(1)}) fusion(f32[256,896]{1,0:T(8,128)} %fusion.13, f32[256,896]{1,0:T(8,128)} %fusion.14, bf16[256,4096]{1,0:T(8,128)(2,1)} %all-gather.5.cloned.1.call-done, bf16[896,4096]{1,0:T(8,128)(2,1)} %param.10), kind=kOutput, calls=%fused_computation.6 | convolution fusion | flops 1882488832 | bytes 12648448 | tf_op jit(solution)/shard_map/dot_general | solution.py:20
  116.9 5.6 %fusion.15 = f32[256,4096]{1,0:T(8,128)S(1)} fusion(bf16[256,896]{1,0:T(8,128)(2,1)S(1)} %get-tuple-element.6, bf16[4096,896]{1,0:T(8,128)(2,1)} %param.8), kind=kOutput, calls=%fused_computation.30 | convolution fusion | flops 1879048192 | bytes 11993088 | tf_op jit(solution)/shard_map/dot_general | solution.py:20
  122.5 3.9 fusion
  126.4 0.0 reduce-scatter.8.cloned.1.call-update
  126.4 0.2 reduce-scatter.6.cloned.1.call-start
  126.6 6.8 %convolution_convert_fusion.2 = bf16[256,4096]{1,0:T(8,128)(2,1)} fusion(bf16[256,896]{1,0:T(8,128)(2,1)S(1)} %get-tuple-element.7, bf16[896,4096]{1,0:T(8,128)(2,1)} %param.10), kind=kOutput, calls=%fused_computation.4 | convolution fusion | flops 1880096768 | bytes 9895936 | tf_op jit(solution)/shard_map/dot_general | solution.py:39
  133.4 0.0 reduce-scatter.6.cloned.1.call-update
  133.5 0.0 reduce-scatter.14.cloned.1.call-start
  133.5 6.7 %convert_bitcast_fusion = bf16[4096,896]{0,1:T(8,128)(2,1)} fusion(bf16[256,896]{1,0:T(8,128)(2,1)S(1)} %get-tuple-element.7, bf16[256,4096]{1,0:T(8,128)(2,1)} %all-gather.5.cloned.1.call-done), kind=kOutput, calls=%fused_computation | convolution fusion | flops 1882718208 | bytes 9895936 | tf_op jit(solution)/shard_map/dot_general | solution.py:14
  140.2 0.0 reduce-scatter.12.cloned.1.call-start
  140.3 5.3 convolution_convert_fusion
  145.6 0.0 reduce-scatter.10.cloned.1.call-start
  145.7 5.4 %convolution_convert_fusion.1 = bf16[4096,896]{1,0:T(8,128)(2,1)} fusion(bf16[256,4096]{1,0:T(8,128)(2,1)S(1)} %copy-done, bf16[256,896]{1,0:T(8,128)(2,1)S(1)} %get-tuple-element.6), kind=kOutput, calls=%fused_computation.2 | convolution fusion | flops 1882718208 | bytes 9895936 | tf_op jit(solution)/shard_map/dot_general | solution.py:14
  151.1 45.3 %reduce-scatter.8.cloned.1.call-done = bf16[16,4096]{1,0:T(8,128)(2,1)} async-done(((bf16[256,4096]{1,0:T(8,128)(2,1)}), bf16[16,4096]{1,0:T(8,128)(2,1)}) %reduce-scatter.8.cloned.1.call-update) | async-done | bytes 131088 | tf_op jit(solution)/shard_map/reduce_scatter | solution.py:54
  196.4 1.1 fusion.6
  197.5 73.2 %reduce-scatter.6.cloned.1.call-done = bf16[16,4096]{1,0:T(8,128)(2,1)} async-done(((bf16[256,4096]{1,0:T(8,128)(2,1)}), bf16[16,4096]{1,0:T(8,128)(2,1)}) %reduce-scatter.6.cloned.1.call-update) | async-done | bytes 131088 | tf_op jit(solution)/shard_map/reduce_scatter | solution.py:38
  270.7 1.8 fusion.10
  272.5 82.8 %reduce-scatter.14.cloned.1.call-done = bf16[512,896]{0,1:T(8,128)(2,1)} async-done(((bf16[4096,896]{0,1:T(8,128)(2,1)}), bf16[512,896]{0,1:T(8,128)(2,1)}) %reduce-scatter.14.cloned.1.call-update) | async-done | bytes 917520 | tf_op jit(solution)/shard_map/reduce_scatter | solution.py:78
  355.3 84.4 %reduce-scatter.12.cloned.1.call-done = bf16[512,896]{1,0:T(8,128)(2,1)} async-done(((bf16[4096,896]{1,0:T(8,128)(2,1)}), bf16[512,896]{1,0:T(8,128)(2,1)}) %reduce-scatter.12.cloned.1.call-update) | async-done | bytes 917520 | tf_op jit(solution)/shard_map/reduce_scatter | solution.py:72
  439.7 84.6 %reduce-scatter.10.cloned.1.call-done = bf16[512,896]{1,0:T(8,128)(2,1)} async-done(((bf16[4096,896]{1,0:T(8,128)(2,1)}), bf16[512,896]{1,0:T(8,128)(2,1)}) %reduce-scatter.10.cloned.1.call-update) | async-done | bytes 917520 | tf_op jit(solution)/shard_map/reduce_scatter | solution.py:66
  (16 shorter events, 0.1 us)
Async XLA Ops:
  7.2 54.0 %all-gather.3.cloned.1.call-start = ((), (), s32[]{:S(2)}) async-start(), calls=%async_computation.5 | async-start | bytes 2228224 | tf_op jit(solution)/shard_map/all_gather | solution.py:33
  10.7 99.3 %all-gather.5.cloned.1.call-start = ((), (), s32[]{:S(2)}) async-start(), calls=%async_computation.7 | async-start | bytes 2228224 | tf_op jit(solution)/shard_map/all_gather | solution.py:45
  11.4 185.0 %reduce-scatter.8.cloned.1.call-start = ((), (), s32[]{:S(2)}) async-start(), calls=%async_computation.8 | async-start | bytes 2228224 | tf_op jit(solution)/shard_map/reduce_scatter | solution.py:54
  61.1 7.1 %copy-start = (bf16[256,4096]{1,0:T(8,128)(2,1)S(1)}, bf16[256,4096]{1,0:T(8,128)(2,1)}, u32[]{:S(2)}) copy-start(bf16[256,4096]{1,0:T(8,128)(2,1)} %all-gather.3.cloned.1.call-done) | copy-start | bytes 6291460
  110.0 12.5 %slice-start = ((s8[7340032]{0:T(1024)(128)(4,1)}), s8[4194304]{0:T(1024)(128)(4,1)S(1)}, s32[]{:S(2)}) async-start(s8[7340032]{0:T(1024)(128)(4,1)} %bitcast.21), calls=%async_computation.12 | async-start | bytes 8388608
  116.9 5.6 %slice-start.1 = ((s8[7340032]{0:T(1024)(128)(4,1)}), s8[3145728]{0:T(1024)(128)(4,1)S(1)}, s32[]{:S(2)}) async-start(s8[7340032]{0:T(1024)(128)(4,1)} %bitcast.21), calls=%async_computation.13 | async-start | bytes 6291456
  126.4 144.3 %reduce-scatter.6.cloned.1.call-start = ((), (), s32[]{:S(2)}) async-start(), calls=%async_computation.6 | async-start | bytes 2228224 | tf_op jit(solution)/shard_map/reduce_scatter | solution.py:38
  133.5 221.8 %reduce-scatter.14.cloned.1.call-start = ((), (), s32[]{:S(2)}) async-start(), calls=%async_computation.11 | async-start | bytes 8257536 | tf_op jit(solution)/shard_map/reduce_scatter | solution.py:78
  140.2 299.5 %reduce-scatter.12.cloned.1.call-start = ((), (), s32[]{:S(2)}) async-start(), calls=%async_computation.10 | async-start | bytes 8257536 | tf_op jit(solution)/shard_map/reduce_scatter | solution.py:72
  145.6 50.8 %copy-start.1 = (bf16[16,4096]{1,0:T(8,128)(2,1)S(1)}, bf16[16,4096]{1,0:T(8,128)(2,1)}, u32[]{:S(2)}) copy-start(bf16[16,4096]{1,0:T(8,128)(2,1)} %param.6) | copy-start | bytes 393220
  145.6 125.1 %copy-start.2 = (bf16[16,4096]{1,0:T(8,128)(2,1)S(1)}, bf16[16,4096]{1,0:T(8,128)(2,1)}, u32[]{:S(2)}) copy-start(bf16[16,4096]{1,0:T(8,128)(2,1)} %param.11) | copy-start | bytes 393220
  145.6 378.6 %reduce-scatter.10.cloned.1.call-start = ((), (), s32[]{:S(2)}) async-start(), calls=%async_computation.9 | async-start | bytes 8257536 | tf_op jit(solution)/shard_map/reduce_scatter | solution.py:66
Sparse Core Ops, SparseCore 0:
  11.0 50.0 all-gather.2
  63.6 46.3 all-gather.4
  126.5 69.8 reduce-scatter.7
  200.6 70.0 reduce-scatter.5
  273.5 81.6 reduce-scatter.13
  358.1 81.5 reduce-scatter.11
  442.7 81.5 reduce-scatter.9
where the time goes:
time: 532 us; the launch traced here: 531 us
  waiting for transfers between devices  456 us (86%)
  matrix products  54 us (10%)
  between operations  14.2 us (3%)
  other arithmetic  6.31 us (1%)
    reduce_scatter x1, waiting for transfers between devices, local(): lax.psum_scatter(first_dim_product(normed_use, d_gate).astype(jnp.bfloat1...  84.6 us
    reduce_scatter x1, waiting for transfers between devices, local(): lax.psum_scatter(first_dim_product(normed_use, d_up).astype(jnp.bfloat16)...  84.4 us
    reduce_scatter x1, waiting for transfers between devices, local(): lax.psum_scatter(first_dim_product(cot_full, hidden_b).astype(jnp.bfloat1...  82.8 us
    reduce_scatter x1, waiting for transfers between devices, local(): lax.psum_scatter(jnp.dot(hidden, w_down, preferred_element_type=jnp.float...  73.2 us
    all_gather x1, waiting for transfers between devices, local(): lax.all_gather(normalized_tokens, 'tensor', axis=0, tiled=True)  49.7 us
    reduce_scatter x1, waiting for transfers between devices, local(): lax.psum_scatter((last_dim_product(d_gate, w_gate) + last_dim_product(d_u...  45.3 us
    all_gather x1, waiting for transfers between devices, local(): cot_full = lax.all_gather(output_cotangent, 'tensor', axis=0, tiled=True)  35.4 us
    dot_general x3, matrix products, first_dim_product(): lax.dot_general(left, right, (((0,), (0,)), ((), ())), preferred_element_...  17.4 us
  transfers between devices with their start and end apart: 7, of which 7 were waited for; matrix products, arithmetic and copies ran while one was open for 8% of the time, Pallas kernels for 0%

commit v1 on v0

v1 whole, which is shorter than its diff:
```python
import jax
import jax.numpy as jnp
from jax import lax
from jax.experimental import pallas as pl
from jax.experimental.pallas import tpu as pltpu
from jax.sharding import PartitionSpec as P

BF = jnp.bfloat16
F32 = jnp.float32
ROWS = 16
REP = 256
D = 4096
FL = 896
SL = 1024
HALF = 512
NX = 4

K_NRM, K_COT, K_SL = 0, 11, 22
K_A2A = 33
K_HID, K_DUP, K_DGT = 36, 40, 44
K_OUT, K_DNM = 48, 53
K_Y = 58
N_SEM = 61


def dot(a, b):
    return jnp.dot(a, b, preferred_element_type=F32)


def dot_t(a, b):
    return lax.dot_general(a, b, (((1,), (1,)), ((), ())), preferred_element_type=F32)


def kernel(
    tok, gain, cot_in, wg_hbm, wu_hbm, wd_hbm,
    lo_out, tig_out, gg_out, gu_out, gd_out,
    wgu, wd, nrm, cot, sl, osl, gu32, dh32, hid, hid_t, dgu, nrm_t,
    lo_part, dn_part, lo_sib, dn_sib, lo_z, dn_z, lo_zs, dn_zs, lo_y, dn_y,
    pg_send, pu_send, pd_send, pg_recv, pu_recv, pd_recv,
    gg_v, gu_v, gd_v, lo_v, tig_v,
    ss, rs, wsem, osem,
):
    dp = lax.axis_index("dp")
    t = lax.axis_index("tensor")
    x = lax.rem(dp, 4)
    yl = lax.div(dp, 4)
    core = lax.rem(t, 2)
    z = lax.rem(lax.div(t, 2), 4)
    yh = lax.div(t, 8)
    z_r, z_l, z_o = lax.rem(z + 1, 4), lax.rem(z + 3, 4), lax.rem(z + 2, 4)
    x_r, x_l, x_o = lax.rem(x + 1, 4), lax.rem(x + 3, 4), lax.rem(x + 2, 4)
    xr, xl, xo = (yl * 4 + x_r, t), (yl * 4 + x_l, t), (yl * 4 + x_o, t)
    yp = ((1 - yl) * 4 + x, t)
    sib = (dp, yh * 8 + z * 2 + (1 - core))
    zr, zl, zo = ((dp, yh * 8 + q * 2 + core) for q in (z_r, z_l, z_o))
    yhp = (dp, (1 - yh) * 8 + z * 2 + core)
    peers = (xr, xl, xo, yp, sib, zr, zl, zo, yhp)

    weights = [
        pltpu.make_async_copy(wg_hbm, wgu.at[:, pl.ds(0, FL)], wsem.at[0]),
        pltpu.make_async_copy(wu_hbm, wgu.at[:, pl.ds(FL, FL)], wsem.at[1]),
        pltpu.make_async_copy(wd_hbm, wd, wsem.at[2]),
    ]
    for w in weights:
        w.start()

    barrier = pltpu.get_barrier_semaphore()
    for dev in peers:
        pl.semaphore_signal(barrier, inc=1, device_id=dev, device_id_type=pl.DeviceIdType.MESH)

    sent = []

    def remote(src, dst, k, dev):
        return pltpu.make_async_remote_copy(
            src_ref=src, dst_ref=dst, send_sem=ss.at[k], recv_sem=rs.at[k],
            device_id=dev, device_id_type=pl.DeviceIdType.MESH,
        )

    def send(src, dst, k, dev):
        copy = remote(src, dst, k, dev)
        copy.start()
        sent.append(copy)

    def got(dst, k):
        remote(dst, dst, k, sib).wait_recv()

    def row(c, zz, y, n=ROWS):
        return pl.multiple_of((c * 8 + zz * 2 + y) * ROWS, n)

    def gather(view, k):
        def put(v, i, dev):
            send(v, v, k + i, dev)

        def s1():
            own = view(row(core, z, yh), ROWS)
            put(own, 0, yhp)
            put(own, 1, zr)
            put(own, 2, zl)

        def s2():
            other = view(row(core, z, 1 - yh), ROWS)
            got(other, k)
            put(other, 3, zr)
            put(other, 4, zl)
            put(view(row(core, z, 0, 32), 32), 5, sib)

        def s3():
            got(view(row(core, z_l, yh), ROWS), k + 1)
            got(view(row(core, z_l, 1 - yh), ROWS), k + 3)
            put(view(row(core, z_l, 0), ROWS), 6, zr)
            put(view(row(core, z_l, 0, 32), 32), 7, sib)
            got(view(row(core, z_r, yh), ROWS), k + 2)
            got(view(row(core, z_r, 1 - yh), ROWS), k + 4)
            put(view(row(core, z_r, 1), ROWS), 8, zl)
            put(view(row(core, z_r, 0, 32), 32), 9, sib)

        def s4():
            got(view(row(core, z_o, 0), ROWS), k + 6)
            got(view(row(core, z_o, 1), ROWS), k + 8)
            put(view(row(core, z_o, 0, 32), 32), 10, sib)

        def s5():
            for i, q in ((5, z), (7, z_l), (9, z_r), (10, z_o)):
                got(view(row(1 - core, q, 0, 32), 32), k + i)

        return s1, s2, s3, s4, s5

    n1, n2, n3, n4, n5 = gather(lambda r, n: nrm.at[pl.ds(r, n), :], K_NRM)
    c1, c2, c3, c4, c5 = gather(lambda r, n: cot.at[pl.ds(r, n), :], K_COT)
    s1, s2, s3, s4, s5 = gather(
        lambda r, n: sl.at[pl.ds(1, 3), :, pl.ds(r, n), :], K_SL
    )

    def along_x(block, half, k):
        def a1():
            send(block(0), block(3), k, xr)
            send(block(0), block(1), k + 1, xl)

        def a2():
            got(block(3), k)
            send(half(3, 0), half(2, 0), k + 2, xr)
            got(block(1), k + 1)
            send(half(1, 1), half(2, 1), k + 3, xl)

        def a3():
            got(half(2, 0), k + 2)
            got(half(2, 1), k + 3)

        return a1, a2, a3

    h1, h2, h3 = along_x(
        lambda s: hid_t.at[:, pl.ds(s * REP, REP)],
        lambda s, i: hid_t.at[pl.ds(i * (FL // 2), FL // 2), pl.ds(s * REP, REP)],
        K_HID,
    )

    def gate_side(at, k):
        return along_x(
            lambda s: dgu.at[pl.ds(s * REP, REP), pl.ds(at, FL)],
            lambda s, i: dgu.at[pl.ds(s * REP + i * 128, 128), pl.ds(at, FL)],
            k,
        )

    u1, u2, u3 = gate_side(FL, K_DUP)
    g1, g2, g3 = gate_side(0, K_DGT)

    def reduce(part, by_core, by_z, z_sum, by_y, k):
        def r1():
            send(part.at[pl.ds(pl.multiple_of((1 - core) * 128, 128), 128), :], by_core, k, sib)

        def r2():
            got(by_core, k)
            base = core * 128

            @pl.loop(0, 4)
            def _(i):
                at = pl.ds(pl.multiple_of(base + i * 32, 32), 32)
                part[at, :] = (
                    part[at, :].astype(F32)
                    + by_core[pl.ds(pl.multiple_of(i * 32, 32), 32), :].astype(F32)
                ).astype(BF)

            for i, (q, dev) in enumerate(((z_r, zr), (z_l, zl), (z_o, zo))):
                at = pl.ds(pl.multiple_of(base + q * 32, 32), 32)
                send(part.at[at, :], by_z.at[i], k + 1 + i, dev)

        def r3():
            for i in range(3):
                got(by_z.at[i], k + 1 + i)
            at = pl.ds(pl.multiple_of(core * 128 + z * 32, 32), 32)
            z_sum[...] = (
                part[at, :].astype(F32)
                + by_z[0].astype(F32)
                + by_z[1].astype(F32)
                + by_z[2].astype(F32)
            ).astype(BF)
            send(z_sum.at[pl.ds(pl.multiple_of((1 - yh) * ROWS, ROWS), ROWS), :], by_y, k + 4, yhp)

        def r4():
            got(by_y, k + 4)
            own = z_sum[pl.ds(pl.multiple_of(yh * ROWS, ROWS), ROWS), :]
            return own.astype(F32) + by_y[...].astype(F32)

        return r1, r2, r3, r4

    o1, o2, o3, o4 = reduce(lo_part, lo_sib, lo_z, lo_zs, lo_y, K_OUT)
    d1, d2, d3, d4 = reduce(dn_part, dn_sib, dn_z, dn_zs, dn_y, K_DNM)

    own = pl.ds(row(core, z, yh), ROWS)
    tokens = tok[...].astype(F32)
    rscale = lax.rsqrt(jnp.mean(tokens * tokens, axis=-1, keepdims=True) + 1e-5)
    gains = gain[...].astype(F32)
    normed = (tokens * rscale * gains).astype(BF)
    nrm[own, :] = normed
    cot[own, :] = cot_in[...]

    pl.semaphore_wait(barrier, len(peers))
    n1()
    c1()
    for q in range(NX):
        for j in range(2):
            lanes = pl.ds(j * 2048 + q * HALF, HALF)
            osl[q, 0, :, pl.ds(j * HALF, HALF)] = nrm[own, lanes]
            osl[q, 1, :, pl.ds(j * HALF, HALF)] = cot_in[:, lanes]
    for i, (q, dev, slot) in enumerate(((x_r, xr, 3), (x_l, xl, 1), (x_o, xo, 2))):
        send(osl.at[q], sl.at[slot, :, own, :], K_A2A + i, dev)

    n2()
    c2()
    n3()
    c3()
    n4()
    for i, slot in enumerate((3, 1, 2)):
        got(sl.at[slot, :, own, :], K_A2A + i)
    n5()
    weights[0].wait()
    weights[1].wait()

    def gate_up(i):
        at = pl.ds(pl.multiple_of(i * 256, 256), 256)
        gu32[:, at] = dot(nrm[...], wgu[:, at])

    pl.loop(0, 3)(gate_up)
    c4()
    s1()
    pl.loop(3, 7)(gate_up)

    @pl.loop(0, REP // 32)
    def _(i):
        at = pl.ds(pl.multiple_of(i * 32, 32), 32)
        gate, up = gu32[at, pl.ds(0, FL)], gu32[at, pl.ds(FL, FL)]
        hid[at, :] = (gate * jax.nn.sigmoid(gate) * up).astype(BF)

    hid_t[:, pl.ds(0, REP)] = hid[...].T
    h1()
    s2()
    c5()
    weights[2].wait()

    @pl.loop(0, 3)
    def _(i):
        at = pl.ds(pl.multiple_of(i * 256, 256), 256)
        dh32[:, at] = dot_t(cot[...], wd[at, :])

    dh32[:, pl.ds(768, 128)] = dot_t(cot[...], wd[pl.ds(768, 128), :])

    @pl.loop(0, REP // 32)
    def _(i):
        at = pl.ds(pl.multiple_of(i * 32, 32), 32)
        gate, up = gu32[at, pl.ds(0, FL)], gu32[at, pl.ds(FL, FL)]
        dh = dh32[at, :]
        sig = jax.nn.sigmoid(gate)
        dgu[at, pl.ds(0, FL)] = (dh * up * sig * (1.0 + gate * (1.0 - sig))).astype(BF)
        dgu[at, pl.ds(FL, FL)] = (dh * (gate * sig)).astype(BF)

    u1()
    g1()
    s3()
    h2()

    @pl.loop(0, D // 512)
    def _(i):
        at = pl.ds(pl.multiple_of(i * 512, 512), 512)
        lo_part[:, at] = dot(hid[...], wd[:, at]).astype(BF)

    o1()
    s4()

    @pl.loop(0, D // 512)
    def _(i):
        at = pl.ds(pl.multiple_of(i * 512, 512), 512)
        dn_part[:, at] = dot_t(dgu[pl.ds(0, REP), :], wgu[at, :]).astype(BF)

    d1()
    u2()
    o2()
    g2()
    for j in range(2):
        lanes = pl.ds(pl.multiple_of(j * 2048 + x * HALF, HALF), HALF)
        sl[0, 0, :, pl.ds(j * HALF, HALF)] = nrm[:, lanes]
        sl[0, 1, :, pl.ds(j * HALF, HALF)] = cot[:, lanes]
    s5()

    @pl.loop(0, NX)
    def _(r):
        nrm_t[:, pl.ds(pl.multiple_of(r * REP, REP), REP)] = sl[r, 0].T

    d2()
    o3()

    def halves(which):
        return pl.ds(pl.multiple_of(which * HALF, HALF), HALF)

    def grad_down(which):
        acc = None
        for r in range(NX):
            p = dot(hid_t[:, pl.ds(r * REP, REP)], sl[r, 1, :, halves(which)])
            acc = p if acc is None else acc + p
        return acc.astype(BF)

    def grad_side(which, at):
        return dot(nrm_t[halves(which), :], dgu[:, pl.ds(at, FL)]).astype(BF)

    h3()
    pd_send[...] = grad_down(1 - yl)
    send(pd_send, pd_recv, K_Y, yp)
    u3()
    pu_send[...] = grad_side(1 - yl, FL)
    send(pu_send, pu_recv, K_Y + 1, yp)
    d3()
    g3()
    pg_send[...] = grad_side(1 - yl, 0)
    send(pg_send, pg_recv, K_Y + 2, yp)
    gd_v[...] = grad_down(yl)
    gu_v[...] = grad_side(yl, FL)
    gg_v[...] = grad_side(yl, 0)

    out = []

    def leave(v, o, i):
        copy = pltpu.make_async_copy(v, o, osem.at[i])
        copy.start()
        out.append(copy)

    lo_v[...] = (tokens + o4()).astype(BF)
    leave(lo_v, lo_out, 0)
    g = d4() * gains
    xhat = tokens * rscale
    inner = jnp.mean(g * xhat, axis=-1, keepdims=True)
    tig_v[...] = (cot_in[...].astype(F32) + rscale * (g - xhat * inner)).astype(BF)
    leave(tig_v, tig_out, 1)

    for i, (v, recv, o) in enumerate(
        ((gd_v, pd_recv, gd_out), (gu_v, pu_recv, gu_out), (gg_v, pg_recv, gg_out))
    ):
        got(recv, K_Y + i)
        v[...] = (v[...].astype(F32) + recv[...].astype(F32)).astype(BF)
        leave(v, o, 2 + i)
    for copy in sent:
        copy.wait_send()
    for copy in out:
        copy.wait()


def local(tokens, rms_norm_gain, w_gate, w_up, w_down, output_cotangent):
    vmem = pl.BlockSpec(memory_space=pltpu.VMEM)
    hbm = pl.BlockSpec(memory_space=pl.ANY)

    def bf(*shape):
        return pltpu.VMEM(shape, BF)

    call = pl.pallas_call(
        kernel,
        out_shape=[
            jax.ShapeDtypeStruct((ROWS, D), BF),
            jax.ShapeDtypeStruct((ROWS, D), BF),
            jax.ShapeDtypeStruct((HALF, FL), BF),
            jax.ShapeDtypeStruct((HALF, FL), BF),
            jax.ShapeDtypeStruct((FL, HALF), BF),
        ],
        in_specs=[vmem, vmem, vmem, hbm, hbm, hbm],
        out_specs=[hbm] * 5,
        scratch_shapes=[
            bf(D, 2 * FL), bf(FL, D), bf(REP, D), bf(REP, D),
            bf(NX, 2, REP, SL), bf(NX, 2, ROWS, SL),
            pltpu.VMEM((REP, 2 * FL), F32), pltpu.VMEM((REP, FL), F32),
            bf(REP, FL), bf(FL, NX * REP), bf(NX * REP, 2 * FL), bf(SL, NX * REP),
            bf(REP, D), bf(REP, D), bf(128, D), bf(128, D),
            bf(3, 32, D), bf(3, 32, D), bf(32, D), bf(32, D), bf(ROWS, D), bf(ROWS, D),
            bf(HALF, FL), bf(HALF, FL), bf(FL, HALF),
            bf(HALF, FL), bf(HALF, FL), bf(FL, HALF),
            bf(HALF, FL), bf(HALF, FL), bf(FL, HALF),
            bf(ROWS, D), bf(ROWS, D),
            pltpu.SemaphoreType.DMA((N_SEM,)),
            pltpu.SemaphoreType.DMA((N_SEM,)),
            pltpu.SemaphoreType.DMA((3,)),
            pltpu.SemaphoreType.DMA((5,)),
        ],
        compiler_params=pltpu.CompilerParams(
            collective_id=0, has_side_effects=True, vmem_limit_bytes=63 * 1000 * 1000
        ),
        cost_estimate=pl.CostEstimate(
            flops=18 * REP * D * FL, bytes_accessed=6 * D * FL, transcendentals=2 * REP * FL
        ),
    )
    return tuple(
        call(tokens, rms_norm_gain.reshape(1, D), output_cotangent, w_gate, w_up, w_down)
    )


def solution(mesh):
    placed = (
        P(("dp", "tensor"), None),
        P(),
        P(None, "tensor"),
        P(None, "tensor"),
        P("tensor", None),
        P(("dp", "tensor"), None),
    )
    return jax.shard_map(
        local,
        mesh=mesh,
        in_specs=placed,
        out_specs=(
            P(("dp", "tensor"), None),
            P(("dp", "tensor"), None),
            P("dp", "tensor"),
            P("dp", "tensor"),
            P("tensor", "dp"),
        ),
        check_vma=False,
    )
```

time: 532 us -> 150 us (0.28)
  waiting for transfers between devices: 456 us -> 0 us
  Pallas kernels: 0 us -> 137 us
  matrix products: 54 us -> 0 us
  between operations: 14.2 us -> 0.64 us
  local copies, waits for them, and re-layouts: 0.03 us -> 11 us
  other arithmetic: 6.31 us -> 0 us
    reduce_scatter x5 -> x0, waiting for transfers between devices: 370 us -> none  [the longest x1 84.6 us: local(): lax.psum_scatter(first_dim_product(normed_use, d_gate).astype(jnp.bfloat1...]
    pallas_call x0 -> x1, Pallas kernels: none -> 137 us  [local(): call(tokens, rms_norm_gain.reshape(1, D), output_cotangent, w_gate, w_up,...]
    all_gather x2 -> x0, waiting for transfers between devices: 85 us -> none  [the longest x1 49.7 us: local(): lax.all_gather(normalized_tokens, 'tensor', axis=0, tiled=True)]
    dot_general x9 -> x0, matrix products: 54 us -> none  [the longest x3 17.4 us: first_dim_product(): lax.dot_general(left, right, (((0,), (0,)), ((), ())), preferred_element_...]
    unnamed x10 -> x5, local copies, waits for them, and re-layouts: 0.03 us -> 9.64 us
  transfers between devices with their start and end apart: 7 -> 0, of which waited for: 7 -> 0; matrix products, arithmetic and copies ran while one was open for 8% -> 0% of each run, Pallas kernels for 0% -> 0%
where the time goes in v1:
time: 150 us; the launch traced here: 149 us
  Pallas kernels  137 us (91%)
  local copies, waits for them, and re-layouts  11 us (7%)
    pallas_call x1, Pallas kernels, local(): call(tokens, rms_norm_gain.reshape(1, D), output_cotangent, w_gate, w_up,...  137 us
    unnamed x5, local copies, waits for them, and re-layouts  9.64 us

profile of v1, /device:TPU:0, one launch (start us, length us, event | category | flops | bytes accessed | tf_op | source)
XLA Modules:
  0.0 148.9 jit_solution(12289378929921118583)
XLA Ops:
  0.6 1.3 reshape.13.gain
  1.9 137.3 %shard_map.101 = (bf16[16,4096]{1,0:T(8,128)(2,1)}, bf16[16,4096]{1,0:T(8,128)(2,1)}, bf16[512,896]{1,0:T(8,128)(2,1)}, bf16[512,896]{1,0:T(8,128)(2,1)}, bf16[896,512]{1,0:T(8,128)(2,1)}) custom-call(bf16[16,4096]{1,0:T(8,128)(2,1)} %tok.1, bf16[1,4096]{1,0:T(2,128)(2,1)} %reshape.13.gain, bf16[16,4096]{1,0:T(8,128)(2,1)} %cot_in.1, ...), custom_call_target="tpu_custom_call" | custom-call | flops 16911433728 | bytes 22020096 | tf_op jit(solution)/shard_map/pallas_call | solution.py:407
  139.3 1.6 %copy.16 = bf16[16,4096]{1,0:T(8,128)(2,1)} copy(bf16[16,4096]{1,0:T(8,128)(2,1)} %get-tuple-element.10) | data formatting | bytes 262144
  140.8 1.6 %copy.17 = bf16[16,4096]{1,0:T(8,128)(2,1)} copy(bf16[16,4096]{1,0:T(8,128)(2,1)} %get-tuple-element.11) | data formatting | bytes 262144
  142.4 2.2 %copy.18 = bf16[512,896]{1,0:T(8,128)(2,1)} copy(bf16[512,896]{1,0:T(8,128)(2,1)} %get-tuple-element.12) | data formatting | bytes 1835008
  144.6 2.2 %copy.19 = bf16[512,896]{1,0:T(8,128)(2,1)} copy(bf16[512,896]{1,0:T(8,128)(2,1)} %get-tuple-element.13) | data formatting | bytes 1835008
  146.8 2.2 %copy.20 = bf16[896,512]{1,0:T(8,128)(2,1)} copy(bf16[896,512]{1,0:T(8,128)(2,1)} %get-tuple-element.14) | data formatting | bytes 1835008

commit v2 on v1

v2 whole, which is shorter than its diff:
```python
import jax
import jax.numpy as jnp
from jax import lax
from jax.experimental import pallas as pl
from jax.experimental.pallas import tpu as pltpu
from jax.sharding import PartitionSpec as P

BF = jnp.bfloat16
F32 = jnp.float32
ROWS = 16
REP = 256
D = 4096
FL = 896
SL = 1024
HALF = 512
NX = 4

K_NRM, K_COT, K_SLN, K_SLC = 0, 13, 26, 39
K_CUT, K_A2A = 52, 53
K_HA, K_HB, K_PA, K_PB = 56, 60, 64, 68
K_UA, K_UB, K_GA, K_GB = 72, 76, 80, 84
K_OUT, K_DNM = 88, 93
K_HY, K_YUA, K_YUB, K_YGA, K_YGB = 98, 99, 100, 101, 102
N_SEM = 103
WA, WB = 512, 384


def dot(a, b):
    return jnp.dot(a, b, preferred_element_type=F32)


def dot_t(a, b):
    return lax.dot_general(a, b, (((1,), (1,)), ((), ())), preferred_element_type=F32)


def kernel(
    tok, gain, cot_in, wg_hbm, wu_hbm, wd_hbm,
    lo_out, tig_out, gg_out, gu_out, gd_out,
    wgu, wd, nrm, cot, sl, osl, cut, gu32, hid, hid_t, dgu, nrm_t,
    lo_part, dn_part, lo_sib, dn_sib, lo_z, dn_z, lo_zs, dn_zs, lo_y, dn_y,
    pg_send, pu_send, pg_recv, pu_recv,
    gg_v, gu_v, gd_v, lo_v, tig_v,
    ss, rs, wsem, osem,
):
    dp = lax.axis_index("dp")
    t = lax.axis_index("tensor")
    x = lax.rem(dp, 4)
    yl = lax.div(dp, 4)
    core = lax.rem(t, 2)
    z = lax.rem(lax.div(t, 2), 4)
    yh = lax.div(t, 8)
    z_r, z_l, z_o = lax.rem(z + 1, 4), lax.rem(z + 3, 4), lax.rem(z + 2, 4)
    x_r, x_l, x_o = lax.rem(x + 1, 4), lax.rem(x + 3, 4), lax.rem(x + 2, 4)
    xr, xl, xo = (yl * 4 + x_r, t), (yl * 4 + x_l, t), (yl * 4 + x_o, t)
    yp = ((1 - yl) * 4 + x, t)
    sib = (dp, yh * 8 + z * 2 + (1 - core))
    zr, zl, zo = ((dp, yh * 8 + q * 2 + core) for q in (z_r, z_l, z_o))
    yhp = (dp, (1 - yh) * 8 + z * 2 + core)
    peers = (xr, xl, xo, yp, sib, zr, zl, zo, yhp)

    weights = [
        pltpu.make_async_copy(wg_hbm, wgu.at[:, pl.ds(0, FL)], wsem.at[0]),
        pltpu.make_async_copy(wu_hbm, wgu.at[:, pl.ds(FL, FL)], wsem.at[1]),
        pltpu.make_async_copy(wd_hbm, wd, wsem.at[2]),
    ]
    for w in weights:
        w.start()

    barrier = pltpu.get_barrier_semaphore()
    for dev in peers:
        pl.semaphore_signal(barrier, inc=1, device_id=dev, device_id_type=pl.DeviceIdType.MESH)

    sent = []

    def remote(src, dst, k, dev):
        return pltpu.make_async_remote_copy(
            src_ref=src, dst_ref=dst, send_sem=ss.at[k], recv_sem=rs.at[k],
            device_id=dev, device_id_type=pl.DeviceIdType.MESH,
        )

    def send(src, dst, k, dev):
        copy = remote(src, dst, k, dev)
        copy.start()
        sent.append(copy)

    def got(dst, k):
        remote(dst, dst, k, sib).wait_recv()

    def row(c, zz, y, n=ROWS):
        return pl.multiple_of((c * 8 + zz * 2 + y) * ROWS, n)

    def gather(view, part, k):
        def put(v, i, dev):
            send(v, v, k + i, dev)

        def s1y():
            put(view(row(core, z, yh), ROWS), 0, yhp)

        def s1z():
            own = view(row(core, z, yh), ROWS)
            put(own, 1, zr)
            put(own, 2, zl)

        def s2():
            got(view(row(core, z_l, yh), ROWS), k + 1)
            put(part(row(core, z_l, yh), 0), 3, zr)
            got(view(row(core, z_r, yh), ROWS), k + 2)
            put(part(row(core, z_r, yh), 1), 4, zl)

        def s3():
            other = view(row(core, z, 1 - yh), ROWS)
            got(other, k)
            put(other, 5, zr)
            put(other, 6, zl)
            put(view(row(core, z, 0, 32), 32), 7, sib)

        def s4():
            got(view(row(core, z_l, 1 - yh), ROWS), k + 5)
            put(part(row(core, z_l, 1 - yh), 0), 8, zr)
            got(view(row(core, z_r, 1 - yh), ROWS), k + 6)
            put(part(row(core, z_r, 1 - yh), 1), 9, zl)
            put(view(row(core, z_l, 0, 32), 32), 10, sib)
            put(view(row(core, z_r, 0, 32), 32), 11, sib)

        def s5():
            got(part(row(core, z_o, yh), 0), k + 3)
            got(part(row(core, z_o, yh), 1), k + 4)
            got(part(row(core, z_o, 1 - yh), 0), k + 8)
            got(part(row(core, z_o, 1 - yh), 1), k + 9)
            put(view(row(core, z_o, 0, 32), 32), 12, sib)

        def s6():
            for i, q in ((7, z), (10, z_l), (11, z_r), (12, z_o)):
                got(view(row(1 - core, q, 0, 32), 32), k + i)

        return s1y, s1z, s2, s3, s4, s5, s6

    def rows_gather(ref, k):
        return gather(
            lambda r, n: ref.at[pl.ds(r, n), :],
            lambda r, i: ref.at[pl.ds(r, ROWS), pl.ds(i * 2048, 2048)],
            k,
        )

    n1y, n1z, n2, n3, n4, n5, n6 = rows_gather(nrm, K_NRM)
    c1y, c1z, c2, c3, c4, c5, c6 = rows_gather(cot, K_COT)
    a1y, a1z, a2, a3, a4, a5, a6 = gather(
        lambda r, n: sl.at[pl.ds(0, 2), pl.ds(1, 3), pl.ds(r, n), :],
        lambda r, i: sl.at[pl.ds(i, 1), pl.ds(1, 3), pl.ds(r, ROWS), :],
        K_SLN,
    )
    b1y, b1z, b2, b3, b4, b5, b6 = gather(
        lambda r, n: sl.at[pl.ds(2, 2), :, pl.ds(r, n), :],
        lambda r, i: sl.at[pl.ds(2 + i, 1), :, pl.ds(r, ROWS), :],
        K_SLC,
    )

    def along_x(block, half, k):
        def x1():
            send(block(0), block(3), k, xr)
            send(block(0), block(1), k + 1, xl)

        def x2():
            got(block(3), k)
            send(half(3, 0), half(2, 0), k + 2, xr)
            got(block(1), k + 1)
            send(half(1, 1), half(2, 1), k + 3, xl)

        def x3():
            got(half(2, 0), k + 2)
            got(half(2, 1), k + 3)

        return x1, x2, x3

    def hidden_side(plane, at, k):
        def lanes(s):
            return pl.ds((plane * NX + s) * REP, REP)

        return along_x(
            lambda s: hid_t.at[pl.ds(at, 448), lanes(s)],
            lambda s, i: hid_t.at[pl.ds(at + i * 224, 224), lanes(s)],
            k,
        )

    def gate_side(at, n, k):
        return along_x(
            lambda s: dgu.at[pl.ds(s * REP, REP), pl.ds(at, n)],
            lambda s, i: dgu.at[pl.ds(s * REP + i * 128, 128), pl.ds(at, n)],
            k,
        )

    ha1, ha2, ha3 = hidden_side(0, 0, K_HA)
    hb1, hb2, hb3 = hidden_side(0, 448, K_HB)
    pa1, pa2, pa3 = hidden_side(1, 0, K_PA)
    pb1, pb2, pb3 = hidden_side(1, 448, K_PB)
    ua1, ua2, ua3 = gate_side(FL, WA, K_UA)
    ub1, ub2, ub3 = gate_side(FL + WA, WB, K_UB)
    ga1, ga2, ga3 = gate_side(0, WA, K_GA)
    gb1, gb2, gb3 = gate_side(WA, WB, K_GB)

    def reduce(part, by_core, by_z, z_sum, by_y, k):
        def r1():
            send(part.at[pl.ds(pl.multiple_of((1 - core) * 128, 128), 128), :], by_core, k, sib)

        def r2():
            got(by_core, k)
            base = core * 128

            @pl.loop(0, 4)
            def _(i):
                at = pl.ds(pl.multiple_of(base + i * 32, 32), 32)
                part[at, :] = (
                    part[at, :].astype(F32)
                    + by_core[pl.ds(pl.multiple_of(i * 32, 32), 32), :].astype(F32)
                ).astype(BF)

            for i, (q, dev) in enumerate(((z_r, zr), (z_l, zl), (z_o, zo))):
                at = pl.ds(pl.multiple_of(base + q * 32, 32), 32)
                send(part.at[at, :], by_z.at[i], k + 1 + i, dev)

        def r3():
            for i in range(3):
                got(by_z.at[i], k + 1 + i)
            at = pl.ds(pl.multiple_of(core * 128 + z * 32, 32), 32)
            z_sum[...] = (
                part[at, :].astype(F32)
                + by_z[0].astype(F32)
                + by_z[1].astype(F32)
                + by_z[2].astype(F32)
            ).astype(BF)
            send(z_sum.at[pl.ds(pl.multiple_of((1 - yh) * ROWS, ROWS), ROWS), :], by_y, k + 4, yhp)

        def r4():
            got(by_y, k + 4)
            own = z_sum[pl.ds(pl.multiple_of(yh * ROWS, ROWS), ROWS), :]
            return own.astype(F32) + by_y[...].astype(F32)

        return r1, r2, r3, r4

    o1, o2, o3, o4 = reduce(lo_part, lo_sib, lo_z, lo_zs, lo_y, K_OUT)
    d1, d2, d3, d4 = reduce(dn_part, dn_sib, dn_z, dn_zs, dn_y, K_DNM)

    own = pl.ds(row(core, z, yh), ROWS)
    tokens = tok[...].astype(F32)
    rscale = lax.rsqrt(jnp.mean(tokens * tokens, axis=-1, keepdims=True) + 1e-5)
    gains = gain[...].reshape(1, D).astype(F32)
    nrm[own, :] = (tokens * rscale * gains).astype(BF)
    cot[own, :] = cot_in[...]

    pl.semaphore_wait(barrier, len(peers))
    n1y()
    n1z()
    send(cot_in.at[:, pl.ds(pl.multiple_of((1 - yl) * 2048, 2048), 2048)], cut, K_CUT, yp)
    c1y()
    for q in range(NX):
        osl[q, 0] = nrm[own, pl.ds(q * HALF, HALF)]
        osl[q, 1] = nrm[own, pl.ds(2048 + q * HALF, HALF)]
        osl[q, 2] = cot_in[:, pl.ds(pl.multiple_of(yl * 2048 + q * HALF, HALF), HALF)]
    n2()
    n3()
    c1z()
    got(cut, K_CUT)
    for q in range(NX):
        osl[q, 3] = cut[:, pl.ds(q * HALF, HALF)]
    for i, (q, dev, slot) in enumerate(((x_r, xr, 3), (x_l, xl, 1), (x_o, xo, 2))):
        send(osl.at[q], sl.at[:, slot, own, :], K_A2A + i, dev)
    for i in range(2, 4):
        sl[i, 0, own, :] = osl[x, i]
    n4()
    c2()
    c3()
    n5()
    for i, slot in enumerate((3, 1, 2)):
        got(sl.at[:, slot, own, :], K_A2A + i)
    a1y()
    weights[0].wait()
    weights[1].wait()
    n6()

    def gate_up(i):
        at = pl.ds(pl.multiple_of(i * 256, 256), 256)
        gu32[:, at] = dot(nrm[...], wgu[:, at])

    pl.loop(0, 2)(gate_up)
    c4()
    a1z()
    b1y()
    pl.loop(2, 5)(gate_up)
    c5()
    a2()
    a3()
    pl.loop(5, 7)(gate_up)

    @pl.loop(0, REP // 32)
    def _(i):
        at = pl.ds(pl.multiple_of(i * 32, 32), 32)
        gate, up = gu32[at, pl.ds(0, FL)], gu32[at, pl.ds(FL, FL)]
        hid[at, :] = (gate * jax.nn.sigmoid(gate) * up).astype(BF)

    hid_t[:, pl.ds(0, REP)] = hid[...].T
    send(hid_t.at[:, pl.ds(0, REP)], hid_t.at[:, pl.ds(NX * REP, REP)], K_HY, yp)
    ha1()
    c6()
    weights[2].wait()

    def gate_grads(at, n):
        dh = dot_t(cot[...], wd[pl.ds(at, n), :])
        gate, up = gu32[:, pl.ds(at, n)], gu32[:, pl.ds(pl.multiple_of(FL + at, 128), n)]
        sig = jax.nn.sigmoid(gate)
        dgu[pl.ds(0, REP), pl.ds(at, n)] = (
            dh * up * sig * (1.0 + gate * (1.0 - sig))
        ).astype(BF)
        dgu[pl.ds(0, REP), pl.ds(pl.multiple_of(FL + at, 128), n)] = (dh * (gate * sig)).astype(BF)

    @pl.loop(0, 3)
    def _(i):
        gate_grads(pl.multiple_of(i * 256, 256), 256)

    gate_grads(768, 128)
    ua1()
    ub1()

    def layer_tile(i):
        at = pl.ds(pl.multiple_of(i * 512, 512), 512)
        lo_part[:, at] = dot(hid[...], wd[:, at]).astype(BF)

    def normed_tile(i):
        at = pl.ds(pl.multiple_of(i * 512, 512), 512)
        dn_part[:, at] = dot_t(dgu[pl.ds(0, REP), :], wgu[at, :]).astype(BF)

    a4()
    ha2()
    pl.loop(0, 8)(layer_tile)
    o1()
    a5()
    b1z()
    pl.loop(0, 4)(normed_tile)
    ua2()
    ga1()
    o2()
    a6()

    for j in range(2):
        lanes = pl.ds(pl.multiple_of(j * 2048 + x * HALF, HALF), HALF)
        nrm_t[pl.ds(j * HALF, HALF), pl.ds(0, REP)] = nrm[:, lanes].T

    @pl.loop(1, NX)
    def _(r):
        at = pl.ds(pl.multiple_of(r * REP, REP), REP)
        nrm_t[pl.ds(0, HALF), at] = sl[0, r].T
        nrm_t[pl.ds(HALF, HALF), at] = sl[1, r].T

    ub2()
    gb1()

    def halves(which):
        return pl.ds(pl.multiple_of(which * HALF, HALF), HALF)

    def side(which, at, n):
        return dot(nrm_t[halves(which), :], dgu[:, pl.ds(at, n)]).astype(BF)

    ua3()
    pu_send[:, pl.ds(0, WA)] = side(1 - yl, FL, WA)
    send(pu_send.at[:, pl.ds(0, WA)], pu_recv.at[:, pl.ds(0, WA)], K_YUA, yp)
    b2()
    b3()
    ub3()
    pu_send[:, pl.ds(WA, WB)] = side(1 - yl, FL + WA, WB)
    send(pu_send.at[:, pl.ds(WA, WB)], pu_recv.at[:, pl.ds(WA, WB)], K_YUB, yp)
    got(hid_t.at[:, pl.ds(NX * REP, REP)], K_HY)
    hb1()
    pl.loop(4, 8)(normed_tile)
    d1()
    ga2()
    pa1()
    gu_v[...] = side(yl, FL, FL)
    gb2()
    pb1()
    b4()
    d2()
    ga3()
    pg_send[:, pl.ds(0, WA)] = side(1 - yl, 0, WA)
    send(pg_send.at[:, pl.ds(0, WA)], pg_recv.at[:, pl.ds(0, WA)], K_YGA, yp)
    gb3()
    pg_send[:, pl.ds(WA, WB)] = side(1 - yl, WA, WB)
    send(pg_send.at[:, pl.ds(WA, WB)], pg_recv.at[:, pl.ds(WA, WB)], K_YGB, yp)
    hb2()
    o3()
    b5()
    gg_v[...] = side(yl, 0, FL)
    pa2()
    d3()
    b6()

    def down(plane):
        return dot(
            hid_t[:, pl.ds(plane * NX * REP, NX * REP)],
            sl[2 + plane].reshape(NX * REP, HALF),
        )

    ha3()
    hb3()
    gd_v[...] = down(0).astype(BF)
    pb2()

    out = []

    def leave(v, o, i):
        copy = pltpu.make_async_copy(v, o, osem.at[i])
        copy.start()
        out.append(copy)

    lo_v[...] = (tokens + o4()).astype(BF)
    leave(lo_v, lo_out, 0)
    g = d4() * gains
    xhat = tokens * rscale
    inner = jnp.mean(g * xhat, axis=-1, keepdims=True)
    tig_v[...] = (cot_in[...].astype(F32) + rscale * (g - xhat * inner)).astype(BF)
    leave(tig_v, tig_out, 1)

    def finish(v, recv, at, n, k):
        lanes = pl.ds(at, n)
        got(recv.at[:, lanes], k)
        v[:, lanes] = (v[:, lanes].astype(F32) + recv[:, lanes].astype(F32)).astype(BF)

    finish(gu_v, pu_recv, 0, WA, K_YUA)
    finish(gu_v, pu_recv, WA, WB, K_YUB)
    leave(gu_v, gu_out, 2)
    finish(gg_v, pg_recv, 0, WA, K_YGA)
    pa3()
    pb3()
    gd_v[...] = (gd_v[...].astype(F32) + down(1)).astype(BF)
    leave(gd_v, gd_out, 3)
    finish(gg_v, pg_recv, WA, WB, K_YGB)
    leave(gg_v, gg_out, 4)
    for copy in sent:
        copy.wait_send()
    for copy in out:
        copy.wait()


def move(*refs):
    sources, results, held = refs[:5], refs[5:10], refs[10:15]
    sems_in, sems_out = refs[15:]
    ins = [pltpu.make_async_copy(a, v, sems_in.at[i]) for i, (a, v) in enumerate(zip(sources, held))]
    outs = [pltpu.make_async_copy(v, b, sems_out.at[i]) for i, (v, b) in enumerate(zip(held, results))]
    for copy in ins:
        copy.start()
    for arrived, copy in zip(ins, outs):
        arrived.wait()
        copy.start()
    for copy in outs:
        copy.wait()


def local(tokens, rms_norm_gain, w_gate, w_up, w_down, output_cotangent):
    vmem = pl.BlockSpec(memory_space=pltpu.VMEM)
    hbm = pl.BlockSpec(memory_space=pl.ANY)

    def bf(*shape):
        return pltpu.VMEM(shape, BF)

    shapes = [
        jax.ShapeDtypeStruct((ROWS, D), BF),
        jax.ShapeDtypeStruct((ROWS, D), BF),
        jax.ShapeDtypeStruct((HALF, FL), BF),
        jax.ShapeDtypeStruct((HALF, FL), BF),
        jax.ShapeDtypeStruct((FL, HALF), BF),
    ]
    call = pl.pallas_call(
        kernel,
        out_shape=shapes,
        in_specs=[vmem, vmem, vmem, hbm, hbm, hbm],
        out_specs=[hbm] * 5,
        scratch_shapes=[
            bf(D, 2 * FL), bf(FL, D), bf(REP, D), bf(REP, D),
            bf(4, NX, REP, HALF), bf(NX, 4, ROWS, HALF), bf(ROWS, 2048),
            pltpu.VMEM((REP, 2 * FL), F32),
            bf(REP, FL), bf(FL, 2 * NX * REP), bf(NX * REP, 2 * FL), bf(SL, NX * REP),
            bf(REP, D), bf(REP, D), bf(128, D), bf(128, D),
            bf(3, 32, D), bf(3, 32, D), bf(32, D), bf(32, D), bf(ROWS, D), bf(ROWS, D),
            bf(HALF, FL), bf(HALF, FL), bf(HALF, FL), bf(HALF, FL),
            bf(HALF, FL), bf(HALF, FL), bf(FL, HALF),
            bf(ROWS, D), bf(ROWS, D),
            pltpu.SemaphoreType.DMA((N_SEM,)),
            pltpu.SemaphoreType.DMA((N_SEM,)),
            pltpu.SemaphoreType.DMA((3,)),
            pltpu.SemaphoreType.DMA((5,)),
        ],
        compiler_params=pltpu.CompilerParams(
            collective_id=0, has_side_effects=True, vmem_limit_bytes=63 * 1000 * 1000
        ),
        cost_estimate=pl.CostEstimate(
            flops=18 * REP * D * FL, bytes_accessed=6 * D * FL, transcendentals=2 * REP * FL
        ),
    )
    results = call(tokens, rms_norm_gain, output_cotangent, w_gate, w_up, w_down)
    moved = pl.pallas_call(
        move,
        out_shape=shapes,
        in_specs=[hbm] * 5,
        out_specs=[hbm] * 5,
        scratch_shapes=[pltpu.VMEM(a.shape, BF) for a in shapes]
        + [pltpu.SemaphoreType.DMA((5,)), pltpu.SemaphoreType.DMA((5,))],
    )(*results)
    return tuple(moved)


def solution(mesh):
    placed = (
        P(("dp", "tensor"), None),
        P(),
        P(None, "tensor"),
        P(None, "tensor"),
        P("tensor", None),
        P(("dp", "tensor"), None),
    )
    return jax.shard_map(
        local,
        mesh=mesh,
        in_specs=placed,
        out_specs=(
            P(("dp", "tensor"), None),
            P(("dp", "tensor"), None),
            P("dp", "tensor"),
            P("dp", "tensor"),
            P("tensor", "dp"),
        ),
        check_vma=False,
    )
```

time: 150 us -> 113 us (0.75)
  Pallas kernels: 137 us -> 112 us
  local copies, waits for them, and re-layouts: 11 us -> 0 us
    pallas_call x1 -> x2, Pallas kernels: 137 us -> 112 us  [the longest x1 109 us: local(): call(tokens, rms_norm_gain, output_cotangent, w_gate, w_up, w_down)]
    unnamed x5 -> x0, local copies, waits for them, and re-layouts: 9.64 us -> none
where the time goes in v2:
time: 113 us
  Pallas kernels  112 us (99%)
    pallas_call x1, Pallas kernels, local(): call(tokens, rms_norm_gain, output_cotangent, w_gate, w_up, w_down)  109 us
    pallas_call x1, Pallas kernels, local(): pl.pallas_call(move, out_shape=shapes, in_specs=[hbm] * 5, out_specs=[hbm...  2.98 us

profile of v2, /device:TPU:0, one launch (start us, length us, event | category | flops | bytes accessed | tf_op | source)
XLA Modules:
  0.0 112.8 jit_solution(1241346618045132034)
XLA Ops:
  0.6 109.2 %shard_map.101 = (bf16[16,4096]{1,0:T(8,128)(2,1)}, bf16[16,4096]{1,0:T(8,128)(2,1)}, bf16[512,896]{1,0:T(8,128)(2,1)}, bf16[512,896]{1,0:T(8,128)(2,1)}, bf16[896,512]{1,0:T(8,128)(2,1)}) custom-call(bf16[16,4096]{1,0:T(8,128)(2,1)} %tok.1, bf16[4096]{0:T(1024)(128)(2,1)} %gain.1, bf16[16,4096]{1,0:T(8,128)(2,1)} %cot_in.1, bf16[4096,896]{1,0:T(8,128)(2,1)} %wg_hbm.1, ...), custom_call_target="tpu_custom_call" | custom-call | flops 16911433728 | bytes 22020096 | tf_op jit(solution)/shard_map/pallas_call | solution.py:497
  109.9 3.0 %shard_map.102 = (bf16[16,4096]{1,0:T(8,128)(2,1)}, bf16[16,4096]{1,0:T(8,128)(2,1)}, bf16[512,896]{1,0:T(8,128)(2,1)}, bf16[512,896]{1,0:T(8,128)(2,1)}, bf16[896,512]{1,0:T(8,128)(2,1)}) custom-call(bf16[16,4096]{1,0:T(8,128)(2,1)} %get-tuple-element.10.refs_0_, bf16[16,4096]{1,0:T(8,128)(2,1)} %get-tuple-element.11.refs_1_, ...), custom_call_target="tpu_custom_call" | custom-call | tf_op jit(solution)/shard_map/pallas_call | solution.py:498

commit v3 on v2

v3 whole, which is shorter than its diff:
```python
import jax
import jax.numpy as jnp
from jax import lax
from jax.experimental import pallas as pl
from jax.experimental.pallas import tpu as pltpu
from jax.sharding import PartitionSpec as P

BF = jnp.bfloat16
F32 = jnp.float32
ROWS = 16
REP = 256
D = 4096
FL = 896
SL = 1024
HALF = 512
NX = 4

K_NRM, K_COT, K_SLN, K_SLC = 0, 20, 40, 49
K_CUT, K_A2A = 58, 59
K_H1, K_H2, K_PA, K_PB = 62, 66, 70, 74
K_U1, K_UA, K_UB, K_G1, K_GA, K_GB = 78, 82, 86, 90, 94, 98
K_OUT, K_DNM = 102, 107
K_HY1, K_HY2, K_YUA, K_YUB, K_YGA, K_YGB = 112, 113, 114, 115, 116, 117
N_SEM = 118
GRP = 128
WA, WB = 512, 384


def dot(a, b):
    return jnp.dot(a, b, preferred_element_type=F32)


def dot_t(a, b):
    return lax.dot_general(a, b, (((1,), (1,)), ((), ())), preferred_element_type=F32)


def kernel(
    tok, gain, cot_in, wg_hbm, wu_hbm, wd_hbm,
    lo_out, tig_out, gg_out, gu_out, gd_out,
    wgu, wd, nrm, cot, sl, osl, cut, gu32, hid, hid_t, dgu, nrm_t,
    lo_part, dn_part, lo_sib, dn_sib, lo_z, dn_z, lo_zs, dn_zs, lo_y, dn_y,
    pg_send, pu_send, pg_recv, pu_recv,
    gg_v, gu_v, gd_v, lo_v, tig_v,
    ss, rs, wsem, osem,
):
    dp = lax.axis_index("dp")
    t = lax.axis_index("tensor")
    x = lax.rem(dp, 4)
    yl = lax.div(dp, 4)
    core = lax.rem(t, 2)
    z = lax.rem(lax.div(t, 2), 4)
    yh = lax.div(t, 8)
    z_r, z_l, z_o = lax.rem(z + 1, 4), lax.rem(z + 3, 4), lax.rem(z + 2, 4)
    x_r, x_l, x_o = lax.rem(x + 1, 4), lax.rem(x + 3, 4), lax.rem(x + 2, 4)
    xr, xl, xo = (yl * 4 + x_r, t), (yl * 4 + x_l, t), (yl * 4 + x_o, t)
    yp = ((1 - yl) * 4 + x, t)
    sib = (dp, yh * 8 + z * 2 + (1 - core))
    zr, zl, zo = ((dp, yh * 8 + q * 2 + core) for q in (z_r, z_l, z_o))
    yhp = (dp, (1 - yh) * 8 + z * 2 + core)
    peers = (xr, xl, xo, yp, sib, zr, zl, zo, yhp)

    weights = [
        pltpu.make_async_copy(wg_hbm, wgu.at[:, pl.ds(0, FL)], wsem.at[0]),
        pltpu.make_async_copy(wu_hbm, wgu.at[:, pl.ds(FL, FL)], wsem.at[1]),
        pltpu.make_async_copy(wd_hbm, wd, wsem.at[2]),
    ]
    for w in weights:
        w.start()

    barrier = pltpu.get_barrier_semaphore()
    for dev in peers:
        pl.semaphore_signal(barrier, inc=1, device_id=dev, device_id_type=pl.DeviceIdType.MESH)

    sent = []

    def remote(src, dst, k, dev):
        return pltpu.make_async_remote_copy(
            src_ref=src, dst_ref=dst, send_sem=ss.at[k], recv_sem=rs.at[k],
            device_id=dev, device_id_type=pl.DeviceIdType.MESH,
        )

    def send(src, dst, k, dev):
        copy = remote(src, dst, k, dev)
        copy.start()
        sent.append(copy)

    def got(dst, k):
        remote(dst, dst, k, sib).wait_recv()

    def row(c, zz, y):
        return pl.multiple_of(((y * 2 + c) * 4 + zz) * ROWS, ROWS)

    def gather(view, part, k):
        def put(v, i, dev):
            send(v, v, k + i, dev)

        def p1():
            own = view(row(core, z, yh))
            put(own, 0, zr)
            put(own, 1, zl)
            put(own, 2, sib)

        def q1():
            put(part(row(core, z, yh), 0), 8, yhp)
            put(part(row(core, z, yh), 1), 9, yhp)

        def p2():
            left, right = row(core, z_l, yh), row(core, z_r, yh)
            got(view(left), k)
            put(part(left, 0), 3, zr)
            got(view(right), k + 1)
            put(part(right, 1), 4, zl)
            put(view(left), 5, sib)
            put(view(right), 6, sib)

        def p3():
            far = row(core, z_o, yh)
            got(part(far, 0), k + 3)
            got(part(far, 1), k + 4)
            put(view(far), 7, sib)

        def p4():
            for i, q in ((2, z), (5, z_l), (6, z_r), (7, z_o)):
                got(view(row(1 - core, q, yh)), k + i)

        def q2():
            other = row(core, z, 1 - yh)
            for i in range(2):
                got(part(other, i), k + 8 + i)
                put(part(other, i), 10 + i, zr)
                put(part(other, i), 12 + i, zl)
            put(view(other), 14, sib)

        def q3():
            left, right = row(core, z_l, 1 - yh), row(core, z_r, 1 - yh)
            got(part(left, 0), k + 10)
            put(part(left, 0), 15, zr)
            got(part(right, 1), k + 13)
            put(part(right, 1), 16, zl)
            got(part(left, 1), k + 11)
            got(part(right, 0), k + 12)
            put(view(left), 17, sib)
            put(view(right), 18, sib)

        def q4():
            far = row(core, z_o, 1 - yh)
            got(part(far, 0), k + 15)
            got(part(far, 1), k + 16)
            put(view(far), 19, sib)

        def q5():
            for i, q in ((14, z), (17, z_l), (18, z_r), (19, z_o)):
                got(view(row(1 - core, q, 1 - yh)), k + i)

        return p1, p2, p3, p4, q1, q2, q3, q4, q5

    def rows_gather(ref, k):
        return gather(
            lambda r: ref.at[pl.ds(r, ROWS), :],
            lambda r, i: ref.at[pl.ds(r, ROWS), pl.ds(i * 2048, 2048)],
            k,
        )

    np1, np2, np3, np4, nq1, nq2, nq3, nq4, nq5 = rows_gather(nrm, K_NRM)
    cp1, cp2, cp3, cp4, cq1, cq2, cq3, cq4, cq5 = rows_gather(cot, K_COT)
    def slow_gather(view, k):
        def put(v, i, dev):
            send(v, v, k + i, dev)

        def t1():
            own = view(row(core, z, yh), ROWS)
            put(own, 4, yhp)
            put(own, 0, zr)
            put(own, 1, zl)
            put(own, 2, zo)

        def t2():
            other = view(row(core, z, 1 - yh), ROWS)
            got(other, k + 4)
            put(other, 5, zr)
            put(other, 6, zl)
            put(other, 7, zo)

        def t3():
            for i, q in enumerate((z_l, z_r, z_o)):
                got(view(row(core, q, yh), ROWS), k + i)
            put(view(row(core, 0, yh), 64), 3, sib)

        def t4():
            for i, q in enumerate((z_l, z_r, z_o)):
                got(view(row(core, q, 1 - yh), ROWS), k + 5 + i)
            put(view(row(core, 0, 1 - yh), 64), 8, sib)

        def t5():
            got(view(row(1 - core, 0, yh), 64), k + 3)
            got(view(row(1 - core, 0, 1 - yh), 64), k + 8)

        return t1, t2, t3, t4, t5

    a1, a2, a3, a4, a5 = slow_gather(
        lambda r, n: sl.at[pl.ds(0, 2), pl.ds(1, 3), pl.ds(r, n), :], K_SLN
    )
    b1, b2, b3, b4, b5 = slow_gather(
        lambda r, n: sl.at[pl.ds(2, 2), :, pl.ds(r, n), :], K_SLC
    )

    def along_x(block, half, k):
        def x1():
            send(block(0), block(3), k, xr)
            send(block(0), block(1), k + 1, xl)

        def x2():
            got(block(3), k)
            send(half(3, 0), half(2, 0), k + 2, xr)
            got(block(1), k + 1)
            send(half(1, 1), half(2, 1), k + 3, xl)

        def x3():
            got(half(2, 0), k + 2)
            got(half(2, 1), k + 3)

        return x1, x2, x3

    groups = (yh, 1 - yh)

    def group(g):
        return pl.ds(pl.multiple_of(groups[g] * GRP, GRP), GRP)

    def group_lanes(plane, s, g):
        return pl.ds(pl.multiple_of((plane * NX + s) * REP + groups[g] * GRP, GRP), GRP)

    def hidden_group(g, k):
        return along_x(
            lambda s: hid_t.at[:, group_lanes(0, s, g)],
            lambda s, i: hid_t.at[pl.ds(i * 448, 448), group_lanes(0, s, g)],
            k,
        )

    def hidden_partner(at, k):
        def lanes(s):
            return pl.ds((NX + s) * REP, REP)

        return along_x(
            lambda s: hid_t.at[pl.ds(at, 448), lanes(s)],
            lambda s, i: hid_t.at[pl.ds(at + i * 224, 224), lanes(s)],
            k,
        )

    def gate_side(g, at, n, k):
        def rows(s, skip, count):
            return pl.ds(pl.multiple_of(s * REP + groups[g] * GRP + skip, 64), count)

        return along_x(
            lambda s: dgu.at[rows(s, 0, GRP), pl.ds(at, n)],
            lambda s, i: dgu.at[rows(s, i * 64, 64), pl.ds(at, n)],
            k,
        )

    h11, h12, h13 = hidden_group(0, K_H1)
    h21, h22, h23 = hidden_group(1, K_H2)
    pa1, pa2, pa3 = hidden_partner(0, K_PA)
    pb1, pb2, pb3 = hidden_partner(448, K_PB)
    u1, u2, u3 = gate_side(0, FL, FL, K_U1)
    ua1, ua2, ua3 = gate_side(1, FL, WA, K_UA)
    ub1, ub2, ub3 = gate_side(1, FL + WA, WB, K_UB)
    g1, g2, g3 = gate_side(0, 0, FL, K_G1)
    ga1, ga2, ga3 = gate_side(1, 0, WA, K_GA)
    gb1, gb2, gb3 = gate_side(1, WA, WB, K_GB)

    def reduce(part, by_core, by_z, z_sum, by_y, k):
        def r1():
            send(part.at[:, 1 - core], by_core, k, sib)

        def r2():
            got(by_core, k)
            for y in range(2):
                for i in range(2):
                    at = pl.ds(i * 32, 32)
                    part[y, core, at, :] = (
                        part[y, core, at, :].astype(F32) + by_core[y, at, :].astype(F32)
                    ).astype(BF)
            for i, (q, dev) in enumerate(((z_r, zr), (z_l, zl), (z_o, zo))):
                at = pl.ds(pl.multiple_of(q * ROWS, ROWS), ROWS)
                send(part.at[:, core, at, :], by_z.at[i], k + 1 + i, dev)

        def r3():
            for i in range(3):
                got(by_z.at[i], k + 1 + i)
            at = pl.ds(pl.multiple_of(z * ROWS, ROWS), ROWS)
            for y in range(2):
                z_sum[y] = (
                    part[y, core, at, :].astype(F32)
                    + by_z[0, y].astype(F32)
                    + by_z[1, y].astype(F32)
                    + by_z[2, y].astype(F32)
                ).astype(BF)
            send(z_sum.at[1 - yh], by_y, k + 4, yhp)

        def r4():
            got(by_y, k + 4)
            return z_sum[yh].astype(F32) + by_y[...].astype(F32)

        return r1, r2, r3, r4

    o1, o2, o3, o4 = reduce(lo_part, lo_sib, lo_z, lo_zs, lo_y, K_OUT)
    d1, d2, d3, d4 = reduce(dn_part, dn_sib, dn_z, dn_zs, dn_y, K_DNM)

    own = pl.ds(row(core, z, yh), ROWS)
    tokens = tok[...].astype(F32)
    rscale = lax.rsqrt(jnp.mean(tokens * tokens, axis=-1, keepdims=True) + 1e-5)
    gains = gain[...].reshape(1, D).astype(F32)
    nrm[own, :] = (tokens * rscale * gains).astype(BF)
    cot[own, :] = cot_in[...]

    pl.semaphore_wait(barrier, len(peers))
    np1()
    nq1()
    for q in range(NX):
        osl[q, 0] = nrm[own, pl.ds(q * HALF, HALF)]
        osl[q, 1] = nrm[own, pl.ds(2048 + q * HALF, HALF)]
        osl[q, 2] = cot_in[:, pl.ds(pl.multiple_of(yl * 2048 + q * HALF, HALF), HALF)]
    np2()
    cp1()
    nq2()
    cq1()
    send(cot_in.at[:, pl.ds(pl.multiple_of((1 - yl) * 2048, 2048), 2048)], cut, K_CUT, yp)
    np3()
    weights[0].wait()
    weights[1].wait()
    np4()

    def gate_up(g):
        def tile(i):
            at = pl.ds(pl.multiple_of(i * 256, 256), 256)
            gu32[group(g), at] = dot(nrm[group(g), :], wgu[:, at])

        return tile

    def make_hidden(g):
        @pl.loop(0, GRP // 32)
        def _(i):
            at = pl.ds(pl.multiple_of(groups[g] * GRP + i * 32, 32), 32)
            gate, up = gu32[at, pl.ds(0, FL)], gu32[at, pl.ds(FL, FL)]
            hid[at, :] = (gate * jax.nn.sigmoid(gate) * up).astype(BF)

        hid_t[:, group_lanes(0, 0, g)] = hid[group(g), :].T

    def hidden_to_pair(g, k):
        send(hid_t.at[:, group_lanes(0, 0, g)], hid_t.at[:, group_lanes(1, 0, g)], k, yp)

    def make_grads(g):
        rows = group(g)

        def tile(at, n):
            dh = dot_t(cot[rows, :], wd[pl.ds(at, n), :])
            lanes, past = pl.ds(at, n), pl.ds(pl.multiple_of(FL + at, 128), n)
            gate, up = gu32[rows, lanes], gu32[rows, past]
            sig = jax.nn.sigmoid(gate)
            dgu[rows, lanes] = (dh * up * sig * (1.0 + gate * (1.0 - sig))).astype(BF)
            dgu[rows, past] = (dh * (gate * sig)).astype(BF)

        @pl.loop(0, 3)
        def _(i):
            tile(pl.multiple_of(i * 256, 256), 256)

        tile(768, 128)

    pl.loop(0, 3)(gate_up(0))
    cp2()
    nq3()
    got(cut, K_CUT)
    for q in range(NX):
        osl[q, 3] = cut[:, pl.ds(q * HALF, HALF)]
    for i, (q, dev, slot) in enumerate(((x_r, xr, 3), (x_l, xl, 1), (x_o, xo, 2))):
        send(osl.at[q], sl.at[:, slot, own, :], K_A2A + i, dev)
    for i in range(2, 4):
        sl[i, 0, own, :] = osl[x, i]
    pl.loop(3, 7)(gate_up(0))
    cp3()
    cq2()
    make_hidden(0)
    h11()
    hidden_to_pair(0, K_HY1)
    nq4()
    cp4()
    weights[2].wait()
    make_grads(0)
    u1()
    for i, slot in enumerate((3, 1, 2)):
        got(sl.at[:, slot, own, :], K_A2A + i)
    cq3()
    a1()
    nq5()
    h12()
    pl.loop(0, 4)(gate_up(1))
    cq4()
    a2()
    b1()
    pl.loop(4, 7)(gate_up(1))
    u2()
    make_hidden(1)
    hidden_to_pair(1, K_HY2)
    cq5()
    make_grads(1)
    ua1()
    ub1()
    a3()
    a4()

    def layer_tile(i):
        at = pl.ds(pl.multiple_of(i * 512, 512), 512)
        lo_part[:, :, :, at] = dot(hid[...], wd[:, at]).astype(BF).reshape(2, 2, 64, 512)

    def normed_tile(i):
        at = pl.ds(pl.multiple_of(i * 512, 512), 512)
        dn_part[:, :, :, at] = (
            dot_t(dgu[pl.ds(0, REP), :], wgu[at, :]).astype(BF).reshape(2, 2, 64, 512)
        )

    pl.loop(0, 8)(layer_tile)
    o1()
    ua2()
    ub2()
    g1()

    for j in range(2):
        lanes = pl.ds(pl.multiple_of(j * 2048 + x * HALF, HALF), HALF)
        nrm_t[pl.ds(j * HALF, HALF), pl.ds(0, REP)] = nrm[:, lanes].T

    a5()

    @pl.loop(1, NX)
    def _(r):
        at = pl.ds(pl.multiple_of(r * REP, REP), REP)
        nrm_t[pl.ds(0, HALF), at] = sl[0, r].T
        nrm_t[pl.ds(HALF, HALF), at] = sl[1, r].T

    def halves(which):
        return pl.ds(pl.multiple_of(which * HALF, HALF), HALF)

    def side(which, at, n):
        return dot(nrm_t[halves(which), :], dgu[:, pl.ds(at, n)]).astype(BF)

    u3()
    ua3()
    pu_send[:, pl.ds(0, WA)] = side(1 - yl, FL, WA)
    send(pu_send.at[:, pl.ds(0, WA)], pu_recv.at[:, pl.ds(0, WA)], K_YUA, yp)
    ub3()
    pu_send[:, pl.ds(WA, WB)] = side(1 - yl, FL + WA, WB)
    send(pu_send.at[:, pl.ds(WA, WB)], pu_recv.at[:, pl.ds(WA, WB)], K_YUB, yp)
    o2()
    ga1()
    gb1()
    g2()
    b2()
    pl.loop(0, 4)(normed_tile)
    ga2()
    pl.loop(4, 8)(normed_tile)
    d1()
    gb2()
    h21()
    b3()
    g3()
    ga3()
    pg_send[:, pl.ds(0, WA)] = side(1 - yl, 0, WA)
    send(pg_send.at[:, pl.ds(0, WA)], pg_recv.at[:, pl.ds(0, WA)], K_YGA, yp)
    gb3()
    pg_send[:, pl.ds(WA, WB)] = side(1 - yl, WA, WB)
    send(pg_send.at[:, pl.ds(WA, WB)], pg_recv.at[:, pl.ds(WA, WB)], K_YGB, yp)
    d2()
    got(hid_t.at[:, group_lanes(1, 0, 0)], K_HY1)
    got(hid_t.at[:, group_lanes(1, 0, 1)], K_HY2)
    pa1()
    pb1()
    h22()
    b4()
    o3()
    gu_v[...] = side(yl, FL, FL)
    pa2()
    gg_v[...] = side(yl, 0, FL)
    pb2()
    d3()
    b5()

    def down(plane):
        return dot(
            hid_t[:, pl.ds(plane * NX * REP, NX * REP)],
            sl[2 + plane].reshape(NX * REP, HALF),
        )

    h13()
    h23()
    gd_v[...] = down(0).astype(BF)

    out = []

    def leave(v, o, i):
        copy = pltpu.make_async_copy(v, o, osem.at[i])
        copy.start()
        out.append(copy)

    lo_v[...] = (tokens + o4()).astype(BF)
    leave(lo_v, lo_out, 0)
    g = d4() * gains
    xhat = tokens * rscale
    inner = jnp.mean(g * xhat, axis=-1, keepdims=True)
    tig_v[...] = (cot_in[...].astype(F32) + rscale * (g - xhat * inner)).astype(BF)
    leave(tig_v, tig_out, 1)

    def finish(v, recv, at, n, k):
        lanes = pl.ds(at, n)
        got(recv.at[:, lanes], k)
        v[:, lanes] = (v[:, lanes].astype(F32) + recv[:, lanes].astype(F32)).astype(BF)

    finish(gu_v, pu_recv, 0, WA, K_YUA)
    finish(gu_v, pu_recv, WA, WB, K_YUB)
    leave(gu_v, gu_out, 2)
    finish(gg_v, pg_recv, 0, WA, K_YGA)
    pa3()
    pb3()
    gd_v[...] = (gd_v[...].astype(F32) + down(1)).astype(BF)
    leave(gd_v, gd_out, 3)
    finish(gg_v, pg_recv, WA, WB, K_YGB)
    leave(gg_v, gg_out, 4)
    for copy in sent:
        copy.wait_send()
    for copy in out:
        copy.wait()


def move(*refs):
    sources, results, held = refs[:5], refs[5:10], refs[10:15]
    sems_in, sems_out = refs[15:]
    ins = [pltpu.make_async_copy(a, v, sems_in.at[i]) for i, (a, v) in enumerate(zip(sources, held))]
    outs = [pltpu.make_async_copy(v, b, sems_out.at[i]) for i, (v, b) in enumerate(zip(held, results))]
    for copy in ins:
        copy.start()
    for arrived, copy in zip(ins, outs):
        arrived.wait()
        copy.start()
    for copy in outs:
        copy.wait()


def local(tokens, rms_norm_gain, w_gate, w_up, w_down, output_cotangent):
    vmem = pl.BlockSpec(memory_space=pltpu.VMEM)
    hbm = pl.BlockSpec(memory_space=pl.ANY)

    def bf(*shape):
        return pltpu.VMEM(shape, BF)

    shapes = [
        jax.ShapeDtypeStruct((ROWS, D), BF),
        jax.ShapeDtypeStruct((ROWS, D), BF),
        jax.ShapeDtypeStruct((HALF, FL), BF),
        jax.ShapeDtypeStruct((HALF, FL), BF),
        jax.ShapeDtypeStruct((FL, HALF), BF),
    ]
    call = pl.pallas_call(
        kernel,
        out_shape=shapes,
        in_specs=[vmem, vmem, vmem, hbm, hbm, hbm],
        out_specs=[hbm] * 5,
        scratch_shapes=[
            bf(D, 2 * FL), bf(FL, D), bf(REP, D), bf(REP, D),
            bf(4, NX, REP, HALF), bf(NX, 4, ROWS, HALF), bf(ROWS, 2048),
            pltpu.VMEM((REP, 2 * FL), F32),
            bf(REP, FL), bf(FL, 2 * NX * REP), bf(NX * REP, 2 * FL), bf(SL, NX * REP),
            bf(2, 2, 64, D), bf(2, 2, 64, D), bf(2, 64, D), bf(2, 64, D),
            bf(3, 2, ROWS, D), bf(3, 2, ROWS, D), bf(2, ROWS, D), bf(2, ROWS, D), bf(ROWS, D), bf(ROWS, D),
            bf(HALF, FL), bf(HALF, FL), bf(HALF, FL), bf(HALF, FL),
            bf(HALF, FL), bf(HALF, FL), bf(FL, HALF),
            bf(ROWS, D), bf(ROWS, D),
            pltpu.SemaphoreType.DMA((N_SEM,)),
            pltpu.SemaphoreType.DMA((N_SEM,)),
            pltpu.SemaphoreType.DMA((3,)),
            pltpu.SemaphoreType.DMA((5,)),
        ],
        compiler_params=pltpu.CompilerParams(
            collective_id=0, has_side_effects=True, vmem_limit_bytes=63 * 1000 * 1000
        ),
        cost_estimate=pl.CostEstimate(
            flops=18 * REP * D * FL, bytes_accessed=6 * D * FL, transcendentals=2 * REP * FL
        ),
    )
    results = call(tokens, rms_norm_gain, output_cotangent, w_gate, w_up, w_down)
    moved = pl.pallas_call(
        move,
        out_shape=shapes,
        in_specs=[hbm] * 5,
        out_specs=[hbm] * 5,
        scratch_shapes=[pltpu.VMEM(a.shape, BF) for a in shapes]
        + [pltpu.SemaphoreType.DMA((5,)), pltpu.SemaphoreType.DMA((5,))],
    )(*results)
    return tuple(moved)


def solution(mesh):
    placed = (
        P(("dp", "tensor"), None),
        P(),
        P(None, "tensor"),
        P(None, "tensor"),
        P("tensor", None),
        P(("dp", "tensor"), None),
    )
    return jax.shard_map(
        local,
        mesh=mesh,
        in_specs=placed,
        out_specs=(
            P(("dp", "tensor"), None),
            P(("dp", "tensor"), None),
            P("dp", "tensor"),
            P("dp", "tensor"),
            P("tensor", "dp"),
        ),
        check_vma=False,
    )
```

time: 113 us -> 105 us (0.929)
  Pallas kernels: 112 us -> 104 us
    pallas_call x1, Pallas kernels: 109 us -> 101 us  [local(): call(tokens, rms_norm_gain, output_cotangent, w_gate, w_up, w_down)]
where the time goes in v3:
time: 105 us
  Pallas kernels  104 us (99%)
    pallas_call x1, Pallas kernels, local(): call(tokens, rms_norm_gain, output_cotangent, w_gate, w_up, w_down)  101 us
    pallas_call x1, Pallas kernels, local(): pl.pallas_call(move, out_shape=shapes, in_specs=[hbm] * 5, out_specs=[hbm...  2.98 us

profile of v3, /device:TPU:0, one launch (start us, length us, event | category | flops | bytes accessed | tf_op | source)
XLA Modules:
  0.0 104.9 jit_solution(6980389240160396276)
XLA Ops:
  0.6 101.2 %shard_map.101 = (bf16[16,4096]{1,0:T(8,128)(2,1)}, bf16[16,4096]{1,0:T(8,128)(2,1)}, bf16[512,896]{1,0:T(8,128)(2,1)}, bf16[512,896]{1,0:T(8,128)(2,1)}, bf16[896,512]{1,0:T(8,128)(2,1)}) custom-call(bf16[16,4096]{1,0:T(8,128)(2,1)} %tok.1, bf16[4096]{0:T(1024)(128)(2,1)} %gain.1, bf16[16,4096]{1,0:T(8,128)(2,1)} %cot_in.1, bf16[4096,896]{1,0:T(8,128)(2,1)} %wg_hbm.1, ...), custom_call_target="tpu_custom_call" | custom-call | flops 16911433728 | bytes 22020096 | tf_op jit(solution)/shard_map/pallas_call | solution.py:586
  101.8 3.0 %shard_map.102 = (bf16[16,4096]{1,0:T(8,128)(2,1)}, bf16[16,4096]{1,0:T(8,128)(2,1)}, bf16[512,896]{1,0:T(8,128)(2,1)}, bf16[512,896]{1,0:T(8,128)(2,1)}, bf16[896,512]{1,0:T(8,128)(2,1)}) custom-call(bf16[16,4096]{1,0:T(8,128)(2,1)} %get-tuple-element.10.refs_0_, bf16[16,4096]{1,0:T(8,128)(2,1)} %get-tuple-element.11.refs_1_, ...), custom_call_target="tpu_custom_call" | custom-call | tf_op jit(solution)/shard_map/pallas_call | solution.py:587

commit v4 on v3

--- a/solution.py
+++ b/solution.py
@@ -23,7 +23,8 @@
 K_HY1, K_HY2, K_YUA, K_YUB, K_YGA, K_YGB = 112, 113, 114, 115, 116, 117
 N_SEM = 118
 GRP = 128
-WA, WB = 512, 384
+WA, WB = 256, 640
+VA, VB = 640, 256
 
 
 def dot(a, b):
@@ -264,8 +265,8 @@
     ua1, ua2, ua3 = gate_side(1, FL, WA, K_UA)
     ub1, ub2, ub3 = gate_side(1, FL + WA, WB, K_UB)
     g1, g2, g3 = gate_side(0, 0, FL, K_G1)
-    ga1, ga2, ga3 = gate_side(1, 0, WA, K_GA)
-    gb1, gb2, gb3 = gate_side(1, WA, WB, K_GB)
+    ga1, ga2, ga3 = gate_side(1, 0, VA, K_GA)
+    gb1, gb2, gb3 = gate_side(1, VA, VB, K_GB)
 
     def reduce(part, by_core, by_z, z_sum, by_y, k):
         def r1():
@@ -348,7 +349,7 @@
     def hidden_to_pair(g, k):
         send(hid_t.at[:, group_lanes(0, 0, g)], hid_t.at[:, group_lanes(1, 0, g)], k, yp)
 
-    def make_grads(g):
+    def make_grads(g, between=None):
         rows = group(g)
 
         def tile(at, n):
@@ -359,7 +360,11 @@
             dgu[rows, lanes] = (dh * up * sig * (1.0 + gate * (1.0 - sig))).astype(BF)
             dgu[rows, past] = (dh * (gate * sig)).astype(BF)
 
-        @pl.loop(0, 3)
+        tile(0, 256)
+        if between is not None:
+            between()
+
+        @pl.loop(1, 3)
         def _(i):
             tile(pl.multiple_of(i * 256, 256), 256)
 
@@ -401,8 +406,7 @@
     make_hidden(1)
     hidden_to_pair(1, K_HY2)
     cq5()
-    make_grads(1)
-    ua1()
+    make_grads(1, ua1)
     ub1()
     a3()
     a4()
@@ -459,22 +463,22 @@
     d1()
     gb2()
     h21()
-    b3()
-    g3()
-    ga3()
-    pg_send[:, pl.ds(0, WA)] = side(1 - yl, 0, WA)
-    send(pg_send.at[:, pl.ds(0, WA)], pg_recv.at[:, pl.ds(0, WA)], K_YGA, yp)
-    gb3()
-    pg_send[:, pl.ds(WA, WB)] = side(1 - yl, WA, WB)
-    send(pg_send.at[:, pl.ds(WA, WB)], pg_recv.at[:, pl.ds(WA, WB)], K_YGB, yp)
-    d2()
     got(hid_t.at[:, group_lanes(1, 0, 0)], K_HY1)
     got(hid_t.at[:, group_lanes(1, 0, 1)], K_HY2)
     pa1()
     pb1()
+    b3()
+    g3()
+    ga3()
+    o3()
+    pg_send[:, pl.ds(0, VA)] = side(1 - yl, 0, VA)
+    send(pg_send.at[:, pl.ds(0, VA)], pg_recv.at[:, pl.ds(0, VA)], K_YGA, yp)
+    gb3()
+    pg_send[:, pl.ds(VA, VB)] = side(1 - yl, VA, VB)
+    send(pg_send.at[:, pl.ds(VA, VB)], pg_recv.at[:, pl.ds(VA, VB)], K_YGB, yp)
+    d2()
     h22()
     b4()
-    o3()
     gu_v[...] = side(yl, FL, FL)
     pa2()
     gg_v[...] = side(yl, 0, FL)
@@ -499,6 +503,19 @@
         copy.start()
         out.append(copy)
 
+    def finish(v, recv, at, n, k):
+        lanes = pl.ds(at, n)
+        got(recv.at[:, lanes], k)
+        v[:, lanes] = (v[:, lanes].astype(F32) + recv[:, lanes].astype(F32)).astype(BF)
+
+    finish(gu_v, pu_recv, 0, WA, K_YUA)
+    finish(gu_v, pu_recv, WA, WB, K_YUB)
+    leave(gu_v, gu_out, 2)
+    finish(gg_v, pg_recv, 0, VA, K_YGA)
+    pa3()
+    pb3()
+    gd_v[...] = (gd_v[...].astype(F32) + down(1)).astype(BF)
+    leave(gd_v, gd_out, 3)
     lo_v[...] = (tokens + o4()).astype(BF)
     leave(lo_v, lo_out, 0)
     g = d4() * gains
@@ -507,20 +524,7 @@
     tig_v[...] = (cot_in[...].astype(F32) + rscale * (g - xhat * inner)).astype(BF)
     leave(tig_v, tig_out, 1)
 
-    def finish(v, recv, at, n, k):
-        lanes = pl.ds(at, n)
-        got(recv.at[:, lanes], k)
-        v[:, lanes] = (v[:, lanes].astype(F32) + recv[:, lanes].astype(F32)).astype(BF)
-
-    finish(gu_v, pu_recv, 0, WA, K_YUA)
-    finish(gu_v, pu_recv, WA, WB, K_YUB)
-    leave(gu_v, gu_out, 2)
-    finish(gg_v, pg_recv, 0, WA, K_YGA)
-    pa3()
-    pb3()
-    gd_v[...] = (gd_v[...].astype(F32) + down(1)).astype(BF)
-    leave(gd_v, gd_out, 3)
-    finish(gg_v, pg_recv, WA, WB, K_YGB)
+    finish(gg_v, pg_recv, VA, VB, K_YGB)
     leave(gg_v, gg_out, 4)
     for copy in sent:
         copy.wait_send()

time: 105 us -> 102 us (0.971)
  Pallas kernels: 104 us -> 101 us
    pallas_call x1, Pallas kernels: 101 us -> 98 us  [local(): call(tokens, rms_norm_gain, output_cotangent, w_gate, w_up, w_down)]
where the time goes in v4:
time: 102 us
  Pallas kernels  101 us (99%)
    pallas_call x1, Pallas kernels, local(): call(tokens, rms_norm_gain, output_cotangent, w_gate, w_up, w_down)  98 us
    pallas_call x1, Pallas kernels, local(): pl.pallas_call(move, out_shape=shapes, in_specs=[hbm] * 5, out_specs=[hbm...  2.98 us

profile of v4, /device:TPU:0, one launch (start us, length us, event | category | flops | bytes accessed | tf_op | source)
XLA Modules:
  0.0 101.8 jit_solution(71453103870027649)
XLA Ops:
  0.6 98.0 %shard_map.101 = (bf16[16,4096]{1,0:T(8,128)(2,1)}, bf16[16,4096]{1,0:T(8,128)(2,1)}, bf16[512,896]{1,0:T(8,128)(2,1)}, bf16[512,896]{1,0:T(8,128)(2,1)}, bf16[896,512]{1,0:T(8,128)(2,1)}) custom-call(bf16[16,4096]{1,0:T(8,128)(2,1)} %tok.1, bf16[4096]{0:T(1024)(128)(2,1)} %gain.1, bf16[16,4096]{1,0:T(8,128)(2,1)} %cot_in.1, bf16[4096,896]{1,0:T(8,128)(2,1)} %wg_hbm.1, ...), custom_call_target="tpu_custom_call" | custom-call | flops 16911433728 | bytes 22020096 | tf_op jit(solution)/shard_map/pallas_call | solution.py:590
  98.7 3.0 %shard_map.102 = (bf16[16,4096]{1,0:T(8,128)(2,1)}, bf16[16,4096]{1,0:T(8,128)(2,1)}, bf16[512,896]{1,0:T(8,128)(2,1)}, bf16[512,896]{1,0:T(8,128)(2,1)}, bf16[896,512]{1,0:T(8,128)(2,1)}) custom-call(bf16[16,4096]{1,0:T(8,128)(2,1)} %get-tuple-element.10.refs_0_, bf16[16,4096]{1,0:T(8,128)(2,1)} %get-tuple-element.11.refs_1_, ...), custom_call_target="tpu_custom_call" | custom-call | tf_op jit(solution)/shard_map/pallas_call | solution.py:591
